TPU v7x, 32 devices: a whole 2x2x4 slice. The times are simulated.
32 devices in a mesh: eg: 8 (over z, x), blk: 4 (over y, core).
Axes of the slice: x: 2, y: 2, z: 4, core: 2. Of those that a mesh axis runs over, the one named last changes fastest.
Arguments:
- tokens: bfloat16 [256, 7168], P(('eg', 'blk')), may hold values from -6 to 6
- grad_out: bfloat16 [256, 7168], P(('eg', 'blk')), may hold values from -4 to 4
- expert_ids: int32 [256, 2], P(('eg', 'blk')), may hold values from 0 to 7, all different within a row; in each aligned block of 8 rows (0 to 7, 8 to 15, ...) at most 4 rows name the same one
- gate_weights: bfloat16 [256, 2], P(('eg', 'blk')), may hold values from 0.049804688 to 1
- gate_codes: bfloat16 [8, 7168, 2048], P('eg', None, 'blk'), may hold values from -0.0625 to 0.0625
- up_codes: bfloat16 [8, 7168, 2048], P('eg', None, 'blk'), may hold values from -0.0625 to 0.0625
- down_codes: bfloat16 [8, 7168, 2048], P('eg', None, 'blk'), may hold values from -0.125 to 0.125
- block_scales: bfloat16 [8, 3, 16, 56], P('eg', None, 'blk'), may hold values from 0.29882812 to 3
Outputs:
- grad_tokens: bfloat16 [256, 7168], P(('eg', 'blk'))
- grad_gates: bfloat16 [256, 2], P(('eg', 'blk'))
- gate_grad: bfloat16 [8, 7168, 2048], P('eg', None, 'blk')
- up_grad: bfloat16 [8, 7168, 2048], P('eg', None, 'blk')
- down_grad: bfloat16 [8, 7168, 2048], P('eg', None, 'blk')
Inputs may be any that keep to these rules, and one draw needn't show every extreme that they name: `expert_ids`: each token names 2 different experts. Among the 8 tokens of one device (aligned blocks of rows) at most 4 name the same expert, and in every draw some device's tokens reach 4 for some expert.
All inputs are finite; a program needn't handle non-finite values.
Results may differ from a plain program's by a relative error of at most 0.028.
Values may be sent and summed in bfloat16 or wider, within the bound.
A program may use at most 128 MiB of HBM per device.

v0:
```python
import jax
import jax.numpy as jnp
from jax import lax
from jax.sharding import PartitionSpec as P

QBLOCK = 128
TOPK = 2


def dequantize(codes, scales):
    rows_in, cols_in = codes.shape
    blocks = codes.astype(jnp.float32).reshape(rows_in // QBLOCK, QBLOCK, cols_in // QBLOCK, QBLOCK)
    scaled = blocks * jnp.transpose(scales.astype(jnp.float32))[:, None, :, None]
    return scaled.reshape(rows_in, cols_in).astype(jnp.bfloat16)


def backward_math(gate_pre, up_pre, down_back, gates):
    sigma = jax.nn.sigmoid(gate_pre)
    hidden = gate_pre * sigma * up_pre
    grad_hidden = gates[:, None] * down_back
    grad_up = (grad_hidden * gate_pre * sigma).astype(jnp.bfloat16)
    grad_gate = (grad_hidden * up_pre * sigma * (1.0 + gate_pre * (1.0 - sigma))).astype(
        jnp.bfloat16
    )
    gated_hidden = (gates[:, None] * hidden).astype(jnp.bfloat16)
    return (hidden, grad_gate, grad_up, gated_hidden)


def routing_tables(expert_ids, experts, capacity):
    route_hot = (
        expert_ids[:, :, None] == jnp.arange(experts, dtype=jnp.int32)[None, None, :]
    ).astype(jnp.int32)
    chosen = jnp.sum(route_hot, axis=1)
    rows = jnp.arange(expert_ids.shape[0], dtype=jnp.int32)
    before = (rows[None, :] < rows[:, None]).astype(jnp.int32)
    earlier = jnp.sum(before[:, :, None] * chosen[None, :, :], axis=1)
    slot_hot = (earlier[:, :, None] == jnp.arange(capacity, dtype=jnp.int32)[None, None, :]).astype(
        jnp.int32
    )
    placed = chosen[:, :, None] * slot_hot
    picked = route_hot[:, :, :, None] * slot_hot[:, None, :, :]
    return (placed.astype(jnp.float32), picked.astype(jnp.float32))


def project_back(grad_gate, grad_up, wgate, wup):
    contract_cols = (((1,), (1,)), ((), ()))
    partial_value = lax.dot_general(
        grad_gate, wgate, contract_cols, preferred_element_type=jnp.float32
    )
    return partial_value + lax.dot_general(
        grad_up, wup, contract_cols, preferred_element_type=jnp.float32
    )


def row_sum(left, right):
    return lax.dot_general(
        left, right, (((0,), (0,)), ((), ())), preferred_element_type=jnp.float32
    )


def on_device(
    tokens, grad_out, expert_ids, gate_weights, gate_codes, up_codes, down_codes, block_scales
):
    experts = lax.axis_size("eg")
    width = tokens.shape[1]
    capacity = 2 * tokens.shape[0] * TOPK // experts
    placed, picked = routing_tables(expert_ids, experts, capacity)
    placed_low = placed.astype(jnp.bfloat16)
    send_tokens = jnp.einsum(
        "tec,td->ecd", placed_low, tokens, preferred_element_type=jnp.float32
    ).astype(jnp.bfloat16)
    send_cotan = jnp.einsum(
        "tec,td->ecd", placed_low, grad_out, preferred_element_type=jnp.float32
    ).astype(jnp.bfloat16)
    send_gates = jnp.einsum(
        "tkec,tk->ec", picked, gate_weights.astype(jnp.float32), precision=lax.Precision.HIGHEST
    ).astype(jnp.bfloat16)
    recv_tokens, recv_cotan, recv_gates = (
        lax.all_to_all(send_tokens, "eg", split_axis=0, concat_axis=0, tiled=True),
        lax.all_to_all(send_cotan, "eg", split_axis=0, concat_axis=0, tiled=True),
        lax.all_to_all(send_gates, "eg", split_axis=0, concat_axis=0, tiled=True),
    )
    wgate = dequantize(gate_codes[0], block_scales[0, 0])
    wup = dequantize(up_codes[0], block_scales[0, 1])
    wdown = dequantize(down_codes[0], block_scales[0, 2])
    all_tokens, all_cotan, all_gates = (
        lax.all_gather(recv_tokens, "blk", axis=0, tiled=True),
        lax.all_gather(recv_cotan, "blk", axis=0, tiled=True),
        lax.all_gather(recv_gates, "blk", axis=0, tiled=True),
    )
    feats = all_tokens.reshape(-1, width)
    cotan = all_cotan.reshape(-1, width)
    gates = all_gates.reshape(-1).astype(jnp.float32)
    gate_pre = jnp.dot(feats, wgate, preferred_element_type=jnp.float32)
    up_pre = jnp.dot(feats, wup, preferred_element_type=jnp.float32)
    down_back = jnp.dot(cotan, wdown, preferred_element_type=jnp.float32)
    hidden, grad_gate, grad_up, gated_hidden = backward_math(gate_pre, up_pre, down_back, gates)
    contrib = project_back(grad_gate, grad_up, wgate, wup)
    scores = jnp.sum(hidden * down_back, axis=1)
    contrib, scores, grad_gate, grad_up, gated_hidden, feats, cotan = (
        contrib,
        scores,
        grad_gate,
        grad_up,
        gated_hidden,
        feats,
        cotan,
    )
    slots = contrib.shape[0] // capacity
    summed_rows, summed_scores = (
        lax.psum_scatter(
            contrib.reshape(slots, capacity, width).astype(jnp.bfloat16),
            "blk",
            scatter_dimension=0,
            tiled=True,
        ).astype(jnp.float32),
        lax.psum_scatter(
            scores.reshape(slots, capacity).astype(jnp.bfloat16),
            "blk",
            scatter_dimension=0,
            tiled=True,
        ).astype(jnp.float32),
    )
    back_rows = summed_rows.astype(jnp.bfloat16)
    back_gates = summed_scores.astype(jnp.bfloat16)
    gate_grad = row_sum(feats, grad_gate).astype(jnp.bfloat16)[None]
    up_grad = row_sum(feats, grad_up).astype(jnp.bfloat16)[None]
    down_grad = row_sum(cotan, gated_hidden).astype(jnp.bfloat16)[None]
    home_rows, home_gates = (
        lax.all_to_all(back_rows, "eg", split_axis=0, concat_axis=0, tiled=True),
        lax.all_to_all(back_gates, "eg", split_axis=0, concat_axis=0, tiled=True),
    )
    grad_tokens = jnp.einsum(
        "tec,ecd->td", placed_low, home_rows, preferred_element_type=jnp.float32
    ).astype(jnp.bfloat16)
    grad_gates = jnp.einsum(
        "tkec,ec->tk", picked, home_gates.astype(jnp.float32), precision=lax.Precision.HIGHEST
    ).astype(jnp.bfloat16)
    return (grad_tokens, grad_gates, gate_grad, up_grad, down_grad)


def solution(mesh):
    in_specs = (
        P(("eg", "blk"), None),
        P(("eg", "blk"), None),
        P(("eg", "blk"), None),
        P(("eg", "blk"), None),
        P("eg", None, "blk"),
        P("eg", None, "blk"),
        P("eg", None, "blk"),
        P("eg", None, "blk", None),
    )
    out_specs = (
        P(("eg", "blk"), None),
        P(("eg", "blk"), None),
        P("eg", None, "blk"),
        P("eg", None, "blk"),
        P("eg", None, "blk"),
    )
    return jax.shard_map(
        on_device, mesh=mesh, in_specs=in_specs, out_specs=out_specs, check_vma=False
    )
```

profile of v0, /device:TPU:0, one launch (start us, length us, event | category | flops | bytes accessed | tf_op | source)
XLA Modules:
  0.0 231.6 jit_solution(13171636481448807313)
XLA Ops:
  7.2 0.8 fusion.37
  8.1 0.3 convolution_convert_fusion.3
  8.4 1.1 copy.74
  9.5 7.3 %all-to-all-start.2 = ((bf16[8,4,7168]{2,1,0:T(4,128)(2,1)}), bf16[8,4,7168]{2,1,0:T(4,128)(2,1)S(1)}, u32[]{:S(2)}, u32[]{:S(2)}) async-start(bf16[8,4,7168]{2,1,0:T(4,128)(2,1)} %copy.74), calls=%async_computation.2 | async-start | bytes 917504 | tf_op jit(solution)/shard_map/all_to_all | solution.py:79
  16.8 1.2 convolution_convert_fusion.4
  18.0 0.7 convert_bitcast_fusion.2
  18.8 13.7 %reshape.138 = f32[56,128,4,128]{3,2,1,0:T(4,128)} reshape(bf16[1,7168,512]{2,1,0:T(8,128)(2,1)} %param.12) | data formatting | bytes 22020096 | tf_op jit(solution)/shard_map/convert_element_type | solution.py:12
  32.6 13.7 %reshape.137 = f32[56,128,4,128]{3,2,1,0:T(4,128)} reshape(bf16[1,7168,512]{2,1,0:T(8,128)(2,1)} %param.13) | data formatting | bytes 22020096 | tf_op jit(solution)/shard_map/convert_element_type | solution.py:12
  46.3 1.1 copy.71
  47.5 0.1 copy.68
  47.8 0.1 multiply_reduce_fusion.2
  47.9 0.1 copy.115
  48.0 0.7 copy.69
  48.8 13.6 %reshape.136 = f32[56,128,4,128]{3,2,1,0:T(4,128)} reshape(bf16[1,7168,512]{2,1,0:T(8,128)(2,1)} %param.14) | data formatting | bytes 22020096 | tf_op jit(solution)/shard_map/convert_element_type | solution.py:12
  62.4 6.0 %all-to-all-start.1 = ((bf16[8,4,7168]{2,1,0:T(4,128)(2,1)}), bf16[8,4,7168]{2,1,0:T(4,128)(2,1)S(1)}, u32[]{:S(2)}, u32[]{:S(2)}) async-start(bf16[8,4,7168]{2,1,0:T(4,128)(2,1)} %copy.71), calls=%async_computation.1 | async-start | bytes 917504 | tf_op jit(solution)/shard_map/all_to_all | solution.py:80
  68.4 0.7 all-gather.6.cloned.1.call-update
  69.1 9.6 %multiply_convert_fusion = bf16[56,128,4,128]{3,2,1,0:T(4,128)(2,1)} fusion(f32[56,128,4,128]{3,2,1,0:T(4,128)} %reshape.138, f32[56,4]{1,0:T(8,128)S(1)} %copy.76), kind=kLoop, calls=%fused_computation.4 | loop fusion | flops 7340032 | bytes 22020992 | tf_op jit(solution)/shard_map/convert_element_type | solution.py:14
  78.7 9.2 %multiply_convert_fusion.1 = bf16[56,128,4,128]{3,2,1,0:T(4,128)(2,1)} fusion(f32[56,128,4,128]{3,2,1,0:T(4,128)} %reshape.137, f32[56,4]{1,0:T(8,128)S(1)} %copy.75), kind=kLoop, calls=%fused_computation.5 | loop fusion | flops 7340032 | bytes 22020992 | tf_op jit(solution)/shard_map/convert_element_type | solution.py:14
  88.0 6.1 %all-to-all-start = ((bf16[8,1,4]{2,1,0:T(2,128)(2,1)}), bf16[8,1,4]{2,1,0:T(2,128)(2,1)S(1)}, u32[]{:S(2)}, u32[]{:S(2)}) async-start(bf16[8,1,4]{2,1,0:T(2,128)(2,1)} %copy.69), calls=%async_computation | async-start | bytes 8192 | tf_op jit(solution)/shard_map/all_to_all | solution.py:81
  94.1 0.7 all-gather.4.cloned.1.call-update
  94.8 9.6 %multiply_convert_fusion.2 = bf16[56,128,4,128]{3,2,1,0:T(4,128)(2,1)} fusion(f32[56,128,4,128]{3,2,1,0:T(4,128)} %reshape.136, f32[56,4]{1,0:T(8,128)S(1)} %copy.72), kind=kLoop, calls=%fused_computation.6 | loop fusion | flops 7340032 | bytes 22020992 | tf_op jit(solution)/shard_map/convert_element_type | solution.py:14
  104.4 5.2 %all-gather = bf16[32,1,4]{2,1,0:T(2,128)(2,1)S(1)} all-gather(bf16[8,1,4]{2,1,0:T(2,128)(2,1)S(1)} %all-to-all-done), channel_id=2, replica_groups=mesh['eg'=8,'blk'=4] {'blk'}, dimensions={0}, use_global_device_ids=true | all-gather | bytes 320 | tf_op jit(solution)/shard_map/all_gather | solution.py:89
  109.7 0.1 reshape.135
  109.8 2.9 %reshape.134 = bf16[128,7168]{1,0:T(8,128)(2,1)S(1)} reshape(bf16[32,4,7168]{2,1,0:T(4,128)(2,1)} %all-gather.6.cloned.1.call-done) | data formatting | bytes 3670016 | tf_op jit(solution)/shard_map/reshape | solution.py:91
  112.7 4.2 %fusion.10 = f32[128,512]{1,0:T(8,128)S(1)} fusion(bf16[128,7168]{1,0:T(8,128)(2,1)S(1)} %reshape.134, bf16[896,8,4,128]{3,2,1,0:T(4,128)(2,1)} %bitcast.97), kind=kOutput, calls=%fused_computation.20 | convolution fusion | flops 939524096 | bytes 9437184 | tf_op jit(solution)/shard_map/dot_general | solution.py:94
  117.0 4.2 %fusion.13 = f32[128,512]{1,0:T(8,128)S(1)} fusion(bf16[128,7168]{1,0:T(8,128)(2,1)S(1)} %reshape.134, bf16[896,8,4,128]{3,2,1,0:T(4,128)(2,1)} %bitcast.98), kind=kOutput, calls=%fused_computation.23 | convolution fusion | flops 939524096 | bytes 9437184 | tf_op jit(solution)/shard_map/dot_general | solution.py:95
  121.2 3.9 %reshape.133 = bf16[128,7168]{1,0:T(8,128)(2,1)} reshape(bf16[32,4,7168]{2,1,0:T(4,128)(2,1)} %all-gather.4.cloned.1.call-done) | data formatting | bytes 3670016 | tf_op jit(solution)/shard_map/reshape | solution.py:92
  125.2 4.9 %multiply_reduce_fusion = (bf16[128]{0:T(256)(128)(2,1)S(1)}, bf16[128,512]{1,0:T(8,128)(2,1)S(1)}, bf16[128,512]{1,0:T(8,128)(2,1)S(1)}) fusion(f32[128,512]{1,0:T(8,128)S(1)} %fusion.13, f32[128,512]{1,0:T(8,128)S(1)} %fusion.10, f32[128]{0:T(128)S(1)} %reshape.135, bf16[128,7168]{1,0:T(8,128)(2,1)} %reshape.133, bf16[896,8,4,128]{3,2,1,0:T(4,128)(2,1)} %bitcast.99), kind=kOutput, calls=%fused_computation.33 | convolution fusion | flops 940703616 | bytes 9962240 | tf_op jit(solution)/shard_map/dot_general | solution.py:96
  130.1 7.2 %mul.146 = f32[56,128,4,128]{3,2,1,0:T(4,128)} broadcast(f32[56,4]{1,0:T(8,128)S(1)} %copy.76), dimensions={0,2} | broadcast | bytes 14680960 | tf_op jit(solution)/shard_map/mul | solution.py:13
  137.3 11.7 %fusion.7 = f32[128,7168]{1,0:T(8,128)} fusion(bf16[128,512]{1,0:T(8,128)(2,1)S(1)} %get-tuple-element.6, f32[896,8,4,128]{3,2,1,0:T(4,128)} %bitcast.95, bf16[1,7168,512]{2,1,0:T(8,128)(2,1)} %param.12), kind=kOutput, calls=%fused_computation.19 | convolution fusion | flops 950534144 | bytes 25821184 | tf_op jit(solution)/shard_map/dot_general | solution.py:47
  148.9 7.2 %mul.143 = f32[56,128,4,128]{3,2,1,0:T(4,128)} broadcast(f32[56,4]{1,0:T(8,128)S(1)} %copy.75), dimensions={0,2} | broadcast | bytes 14680960 | tf_op jit(solution)/shard_map/mul | solution.py:13
  156.1 12.1 %fusion.5 = bf16[128,7168]{1,0:T(8,128)(2,1)} fusion(f32[128,7168]{1,0:T(8,128)} %fusion.7, bf16[128,512]{1,0:T(8,128)(2,1)S(1)} %get-tuple-element.7, f32[896,8,4,128]{3,2,1,0:T(4,128)} %bitcast.96, bf16[1,7168,512]{2,1,0:T(8,128)(2,1)} %param.13), kind=kOutput, calls=%fused_computation.14 | convolution fusion | flops 952369152 | bytes 27656192 | tf_op jit(solution)/shard_map/dot_general | solution.py:50
  168.2 3.6 %reshape.154 = bf16[32,28672]{1,0:T(8,128)(2,1)} reshape(bf16[128,7168]{1,0:T(8,128)(2,1)} %fusion.5) | data formatting | bytes 3670016
  171.8 0.6 dynamic-slice
  173.0 0.1 convert_element_type.236
  173.1 7.2 %all-reduce = bf16[32,4]{1,0:T(8,128)(2,1)S(1)} all-reduce(bf16[32,4]{1,0:T(8,128)(2,1)S(1)} %convert_element_type.236), channel_id=4, replica_groups=mesh['eg'=8,'blk'=4] {'blk'}, use_global_device_ids=true, to_apply=%region_4.0.clone | all-reduce | flops 128 | bytes 512
  180.4 0.6 copy.81
  181.0 6.0 %all-to-all-start.4 = ((bf16[8,1,4]{2,1,0:T(2,128)(2,1)}), bf16[8,1,4]{2,1,0:T(2,128)(2,1)S(1)}, u32[]{:S(2)}, u32[]{:S(2)}) async-start(bf16[8,1,4]{2,1,0:T(2,128)(2,1)} %copy.81), calls=%async_computation.4 | async-start | bytes 8192 | tf_op jit(solution)/shard_map/all_to_all | solution.py:131
  187.0 5.1 %fusion.2 = bf16[1,7168,512]{2,1,0:T(8,128)(2,1)} fusion(bf16[128,7168]{1,0:T(8,128)(2,1)S(1)} %reshape.134, bf16[128,512]{1,0:T(8,128)(2,1)S(1)} %get-tuple-element.6), kind=kOutput, calls=%fused_computation.10 | convolution fusion | flops 943194112 | bytes 9306112 | tf_op jit(solution)/shard_map/dot_general | solution.py:56
  192.1 11.1 %reduce-scatter.4.cloned.1.call-done = bf16[8,28672]{1,0:T(8,128)(2,1)} async-done(((bf16[32,28672]{1,0:T(8,128)(2,1)}), bf16[8,28672]{1,0:T(8,128)(2,1)}) %reduce-scatter.4.cloned.1.call-update) | async-done | bytes 458768
  203.2 2.1 copy.78
  205.3 5.5 %all-to-all-start.3 = ((bf16[8,4,7168]{2,1,0:T(4,128)(2,1)}), bf16[8,4,7168]{2,1,0:T(4,128)(2,1)S(1)}, u32[]{:S(2)}, u32[]{:S(2)}) async-start(bf16[8,4,7168]{2,1,0:T(4,128)(2,1)} %copy.78), calls=%async_computation.3 | async-start | bytes 917504 | tf_op jit(solution)/shard_map/all_to_all | solution.py:130
  210.9 5.1 %fusion.3 = bf16[1,7168,512]{2,1,0:T(8,128)(2,1)} fusion(bf16[128,7168]{1,0:T(8,128)(2,1)S(1)} %reshape.134, bf16[128,512]{1,0:T(8,128)(2,1)S(1)} %get-tuple-element.7), kind=kOutput, calls=%fused_computation.11 | convolution fusion | flops 943194112 | bytes 9306112 | tf_op jit(solution)/shard_map/dot_general | solution.py:56
  216.0 5.2 %fusion.4 = bf16[1,7168,512]{2,1,0:T(8,128)(2,1)} fusion(bf16[128,7168]{1,0:T(8,128)(2,1)S(1)} %copy-done.2, f32[128]{0:T(128)S(1)} %reshape.135, f32[128,512]{1,0:T(8,128)S(1)} %fusion.13, f32[128,512]{1,0:T(8,128)S(1)} %fusion.10), kind=kOutput, calls=%fused_computation.12 | convolution fusion | flops 943652864 | bytes 9699840 | tf_op jit(solution)/shard_map/dot_general | solution.py:56
  221.4 0.2 multiply_reduce_fusion.1
  221.6 0.6 copy.100
  222.2 1.7 all-to-all-done.3
  224.0 1.1 fusion.6
  (41 shorter events, 1.0 us)
Async XLA Ops:
  7.2 0.9 copy-start
  9.5 52.9 %all-to-all-start.2 = ((bf16[8,4,7168]{2,1,0:T(4,128)(2,1)}), bf16[8,4,7168]{2,1,0:T(4,128)(2,1)S(1)}, u32[]{:S(2)}, u32[]{:S(2)}) async-start(bf16[8,4,7168]{2,1,0:T(4,128)(2,1)} %copy.74), calls=%async_computation.2 | async-start | bytes 917504 | tf_op jit(solution)/shard_map/all_to_all | solution.py:79
  32.6 15.0 %copy-start.5 = (s32[8,2]{0,1:T(2,128)S(1)}, s32[8,2]{0,1:T(2,128)}, u32[]{:S(2)}) copy-start(s32[8,2]{0,1:T(2,128)} %param.10) | copy-start | bytes 196
  32.6 15.0 %copy-start.6 = (bf16[8,2]{0,1:T(2,128)(2,1)S(1)}, bf16[8,2]{0,1:T(2,128)(2,1)}, u32[]{:S(2)}) copy-start(bf16[8,2]{0,1:T(2,128)(2,1)} %param.11) | copy-start | bytes 100
  62.4 6.0 %copy-start.3 = (bf16[8,4,7168]{2,1,0:T(4,128)(2,1)}, bf16[8,4,7168]{2,1,0:T(4,128)(2,1)S(1)}, u32[]{:S(2)}) copy-start(bf16[8,4,7168]{2,1,0:T(4,128)(2,1)S(1)} %all-to-all-done.2) | copy-start | bytes 1376260
  62.4 25.6 %all-to-all-start.1 = ((bf16[8,4,7168]{2,1,0:T(4,128)(2,1)}), bf16[8,4,7168]{2,1,0:T(4,128)(2,1)S(1)}, u32[]{:S(2)}, u32[]{:S(2)}) async-start(bf16[8,4,7168]{2,1,0:T(4,128)(2,1)} %copy.71), calls=%async_computation.1 | async-start | bytes 917504 | tf_op jit(solution)/shard_map/all_to_all | solution.py:80
  68.4 41.4 %all-gather.6.cloned.1.call-start = ((), (), s32[]{:S(2)}) async-start(), calls=%async_computation.7 | async-start | bytes 2293760 | tf_op jit(solution)/shard_map/all_gather | solution.py:87
  88.0 6.1 %copy-start.4 = (bf16[8,4,7168]{2,1,0:T(4,128)(2,1)}, bf16[8,4,7168]{2,1,0:T(4,128)(2,1)S(1)}, u32[]{:S(2)}) copy-start(bf16[8,4,7168]{2,1,0:T(4,128)(2,1)S(1)} %all-to-all-done.1) | copy-start | bytes 1376260
  88.0 16.5 %all-to-all-start = ((bf16[8,1,4]{2,1,0:T(2,128)(2,1)}), bf16[8,1,4]{2,1,0:T(2,128)(2,1)S(1)}, u32[]{:S(2)}, u32[]{:S(2)}) async-start(bf16[8,1,4]{2,1,0:T(2,128)(2,1)} %copy.69), calls=%async_computation | async-start | bytes 8192 | tf_op jit(solution)/shard_map/all_to_all | solution.py:81
  94.0 27.2 %all-gather.4.cloned.1.call-start = ((), (), s32[]{:S(2)}) async-start(), calls=%async_computation.6 | async-start | bytes 2293760 | tf_op jit(solution)/shard_map/all_gather | solution.py:88
  94.8 108.4 %reduce-scatter.4.cloned.1.call-start = ((), (), s32[]{:S(2)}) async-start(), calls=%async_computation.8 | async-start | bytes 2293760
  156.1 15.7 %copy-start.7 = (u32[32]{0:T(128)S(1)}, u32[32]{0:T(128)}, u32[]{:S(2)}) copy-start(u32[32]{0:T(128)} %constant.19) | copy-start | bytes 388
  181.0 24.4 %all-to-all-start.4 = ((bf16[8,1,4]{2,1,0:T(2,128)(2,1)}), bf16[8,1,4]{2,1,0:T(2,128)(2,1)S(1)}, u32[]{:S(2)}, u32[]{:S(2)}) async-start(bf16[8,1,4]{2,1,0:T(2,128)(2,1)} %copy.81), calls=%async_computation.4 | async-start | bytes 8192 | tf_op jit(solution)/shard_map/all_to_all | solution.py:131
  205.3 18.6 %all-to-all-start.3 = ((bf16[8,4,7168]{2,1,0:T(4,128)(2,1)}), bf16[8,4,7168]{2,1,0:T(4,128)(2,1)S(1)}, u32[]{:S(2)}, u32[]{:S(2)}) async-start(bf16[8,4,7168]{2,1,0:T(4,128)(2,1)} %copy.78), calls=%async_computation.3 | async-start | bytes 917504 | tf_op jit(solution)/shard_map/all_to_all | solution.py:130
  210.9 5.2 %copy-start.2 = (bf16[128,7168]{1,0:T(8,128)(2,1)S(1)}, bf16[128,7168]{1,0:T(8,128)(2,1)}, u32[]{:S(2)}) copy-start(bf16[128,7168]{1,0:T(8,128)(2,1)} %reshape.133) | copy-start | bytes 5505028
  210.9 14.2 %copy-start.1 = (bf16[8,7168]{1,0:T(8,128)(2,1)S(1)}, bf16[8,7168]{1,0:T(8,128)(2,1)}, u32[]{:S(2)}) copy-start(bf16[8,7168]{1,0:T(8,128)(2,1)} %param.8) | copy-start | bytes 344068
Sparse Core Ops, SparseCore 0:
  70.8 22.5 all-gather.5
  96.4 22.6 all-gather.3
  171.9 31.2 reduce-scatter.3
where the time goes:
time: 233 us; the launch traced here: 232 us
  local copies, waits for them, and re-layouts  73.7 us (32%)
  matrix products  55.2 us (24%)
  starting transfers between devices  31 us (13%)
  other arithmetic  30.5 us (13%)
  between operations  14.6 us (6%)
  waiting for transfers between devices  14.3 us (6%)
  blocking collectives  12.4 us (5%)
    convert_element_type x3, local copies, waits for them, and re-layouts, dequantize(): codes.astype(jnp.float32)  41 us
    convert_element_type x3, other arithmetic, dequantize(): return scaled.reshape(rows_in, cols_in).astype(jnp.bfloat16)  28.4 us
    dot_general x3, matrix products, row_sum(): lax.dot_general(left, right, (((0,), (0,)), ((), ())), preferred_element_...  15.5 us
    mul x2, local copies, waits for them, and re-layouts, dequantize(): blocks * jnp.transpose(scales.astype(jnp.float32))[:, None, :, None]  14.3 us
    unnamed x4, waiting for transfers between devices  12.5 us
    dot_general x1, matrix products, project_back(): lax.dot_general(grad_up, wup, contract_cols, preferred_element_type=jnp.f...  12.1 us
    dot_general x1, matrix products, project_back(): lax.dot_general(grad_gate, wgate, contract_cols, preferred_element_type=j...  11.7 us
    all_to_all x1, starting transfers between devices, on_device(): lax.all_to_all(send_tokens, 'eg', split_axis=0, concat_axis=0, tiled=True)  7.25 us
  transfers between devices with their start and end apart: 8, of which 2 were waited for; matrix products, arithmetic and copies ran while one was open for 46% of the time, Pallas kernels for 0%

commit v1 on v0

v1 whole, which is shorter than its diff:
```python
import functools

import jax
import jax.numpy as jnp
from jax import lax
from jax.experimental import pallas as pl
from jax.experimental.pallas import tpu as pltpu
from jax.sharding import PartitionSpec as P

QBLOCK = 128
TOPK = 2


def backward_math(gate_pre, up_pre, down_back, gates):
    sigma = jax.nn.sigmoid(gate_pre)
    hidden = gate_pre * sigma * up_pre
    grad_hidden = gates * down_back
    grad_up = (grad_hidden * gate_pre * sigma).astype(jnp.bfloat16)
    grad_gate = (grad_hidden * up_pre * sigma * (1.0 + gate_pre * (1.0 - sigma))).astype(
        jnp.bfloat16
    )
    gated_hidden = (gates * hidden).astype(jnp.bfloat16)
    return (hidden, grad_gate, grad_up, gated_hidden)


def routing_tables(expert_ids, experts, capacity):
    route_hot = (
        expert_ids[:, :, None] == jnp.arange(experts, dtype=jnp.int32)[None, None, :]
    ).astype(jnp.int32)
    chosen = jnp.sum(route_hot, axis=1)
    rows = jnp.arange(expert_ids.shape[0], dtype=jnp.int32)
    before = (rows[None, :] < rows[:, None]).astype(jnp.int32)
    earlier = jnp.sum(before[:, :, None] * chosen[None, :, :], axis=1)
    slot_hot = (earlier[:, :, None] == jnp.arange(capacity, dtype=jnp.int32)[None, None, :]).astype(
        jnp.int32
    )
    placed = chosen[:, :, None] * slot_hot
    picked = route_hot[:, :, :, None] * slot_hot[:, None, :, :]
    return (placed.astype(jnp.float32), picked.astype(jnp.float32))


LANES = 128
NT = (((1,), (1,)), ((), ()))
TN = (((0,), (0,)), ((), ()))
f32, bf16 = jnp.float32, jnp.bfloat16


def expert_kernel(
    steps, x_ref, y_ref, gates_ref, scales_ref, gate_ref, up_ref, down_ref,
    back_ref, dgate_ref, dup_ref, gated_ref,
    wgate, wup, acc_gate, acc_up, acc_down,
):
    j = pl.program_id(0)
    chunk = x_ref.shape[1]
    blocks = chunk // QBLOCK
    hid = gate_ref.shape[2]

    @pl.when(j == 0)
    def _():
        acc_gate[...] = jnp.zeros_like(acc_gate)
        acc_up[...] = jnp.zeros_like(acc_up)
        acc_down[...] = jnp.zeros_like(acc_down)

    def scaled(ref, m):
        parts = []
        for b in range(blocks):
            row = m * blocks + b
            scale = jnp.broadcast_to(scales_ref[0, row : row + 1, :], (QBLOCK, hid)).astype(bf16)
            parts.append(ref[0, b * QBLOCK : (b + 1) * QBLOCK, :] * scale)
        return jnp.concatenate(parts, axis=0)

    place = pl.ds(pl.multiple_of(j * chunk, chunk), chunk)
    wg = scaled(gate_ref, 0)
    wgate[place, :] = wg
    acc_gate[...] += jnp.dot(x_ref[...], wg, preferred_element_type=f32)
    wu = scaled(up_ref, 1)
    wup[place, :] = wu
    acc_up[...] += jnp.dot(x_ref[...], wu, preferred_element_type=f32)
    acc_down[...] += jnp.dot(y_ref[...], scaled(down_ref, 2), preferred_element_type=f32)

    @pl.when(j == steps - 1)
    def _():
        gates = gates_ref[:, 0:1].astype(f32)
        hidden, dgate, dup, gated = backward_math(acc_gate[...], acc_up[...], acc_down[...], gates)
        dgate_ref[...] = dgate
        dup_ref[...] = dup
        gated_ref[...] = gated
        scores = jnp.sum(hidden * acc_down[...], axis=1, keepdims=True)
        width = steps * chunk
        back_ref[:, width : width + LANES] = jnp.broadcast_to(
            scores, (scores.shape[0], LANES)
        ).astype(bf16)

        @pl.loop(0, steps)
        def _(i):
            at = pl.ds(pl.multiple_of(i * chunk, chunk), chunk)
            total = lax.dot_general(dgate_ref[...], wgate[at, :], NT, preferred_element_type=f32)
            total += lax.dot_general(dup_ref[...], wup[at, :], NT, preferred_element_type=f32)
            back_ref[:, at] = total.astype(bf16)


def grads_kernel(x_ref, y_ref, dgate_ref, dup_ref, gated_ref, gate_ref, up_ref, down_ref):
    x = x_ref[...]
    gate_ref[0] = lax.dot_general(x, dgate_ref[...], TN, preferred_element_type=f32).astype(bf16)
    up_ref[0] = lax.dot_general(x, dup_ref[...], TN, preferred_element_type=f32).astype(bf16)
    down_ref[0] = lax.dot_general(
        y_ref[...], gated_ref[...], TN, preferred_element_type=f32
    ).astype(bf16)


def expert_part(rows, scales, gate_codes, up_codes, down_codes, chunk):
    count = rows.shape[0]
    _, width, hid = gate_codes.shape
    steps = width // chunk
    x_spec = pl.BlockSpec((count, chunk), lambda j: (0, j))
    y_spec = pl.BlockSpec((count, chunk), lambda j: (0, steps + j))
    code_spec = pl.BlockSpec((1, chunk, hid), lambda j: (0, j, 0))
    whole = pl.BlockSpec((count, hid), lambda j: (0, 0))
    small = jax.ShapeDtypeStruct((count, hid), bf16)
    return pl.pallas_call(
        functools.partial(expert_kernel, steps),
        grid=(steps,),
        in_specs=[
            x_spec,
            y_spec,
            pl.BlockSpec((count, LANES), lambda j: (0, 2 * width // LANES)),
            pl.BlockSpec((1, scales.shape[1], hid), lambda j: (j, 0, 0)),
            code_spec,
            code_spec,
            code_spec,
        ],
        out_specs=[
            pl.BlockSpec((count, width + LANES), lambda j: (0, 0)),
            whole,
            whole,
            whole,
        ],
        out_shape=[jax.ShapeDtypeStruct((count, width + LANES), bf16), small, small, small],
        scratch_shapes=[pltpu.VMEM((width, hid), bf16)] * 2 + [pltpu.VMEM((count, hid), f32)] * 3,
        compiler_params=pltpu.CompilerParams(vmem_limit_bytes=48 << 20),
        cost_estimate=pl.CostEstimate(
            flops=10 * count * width * hid,
            bytes_accessed=6 * width * hid + 6 * count * width,
            transcendentals=count * hid,
        ),
        name="expert",
    )(rows, rows, rows, scales, gate_codes, up_codes, down_codes)


def grads_part(rows, dgate, dup, gated, width, chunk):
    count, hid = dgate.shape
    steps = width // chunk
    whole = pl.BlockSpec((count, hid), lambda j: (0, 0))
    out = pl.BlockSpec((1, chunk, hid), lambda j: (0, j, 0))
    return pl.pallas_call(
        grads_kernel,
        grid=(steps,),
        in_specs=[
            pl.BlockSpec((count, chunk), lambda j: (0, j)),
            pl.BlockSpec((count, chunk), lambda j: (0, steps + j)),
            whole,
            whole,
            whole,
        ],
        out_specs=[out, out, out],
        out_shape=[jax.ShapeDtypeStruct((1, width, hid), bf16)] * 3,
        compiler_params=pltpu.CompilerParams(vmem_limit_bytes=56 << 20),
        cost_estimate=pl.CostEstimate(
            flops=6 * count * width * hid,
            bytes_accessed=6 * width * hid + 4 * count * width,
            transcendentals=0,
        ),
        name="grads",
    )(rows, rows, dgate, dup, gated)


def on_device(
    tokens, grad_out, expert_ids, gate_weights, gate_codes, up_codes, down_codes, block_scales
):
    experts = lax.axis_size("eg")
    width = tokens.shape[1]
    chunk = max(c for c in range(QBLOCK, 1024 + 1, QBLOCK) if width % c == 0)
    capacity = 2 * tokens.shape[0] * TOPK // experts
    slots = experts * capacity
    placed, picked = routing_tables(expert_ids, experts, capacity)
    flat = placed.astype(bf16).reshape(-1, slots)
    flat_picked = picked.reshape(-1, TOPK, slots)
    gates = jnp.sum(flat_picked * gate_weights.astype(f32)[:, :, None], axis=(0, 1))
    both = jnp.concatenate([tokens, grad_out], axis=1)
    sent = lax.dot_general(flat, both, TN, preferred_element_type=f32).astype(bf16)
    sent = jnp.concatenate(
        [sent, jnp.broadcast_to(gates.astype(bf16)[:, None], (slots, LANES))], axis=1
    )
    received = lax.all_to_all(
        sent.reshape(experts, capacity, -1), "eg", split_axis=0, concat_axis=0, tiled=True
    )
    rows = lax.all_gather(received.reshape(slots, -1), "blk", axis=0, tiled=True)

    hid = gate_codes.shape[2]
    scales = jnp.repeat(jnp.swapaxes(block_scales[0], 1, 2).astype(f32), QBLOCK, axis=2)
    scales = scales.reshape(3, width // chunk, chunk // QBLOCK, hid)
    scales = jnp.swapaxes(scales, 0, 1).reshape(width // chunk, -1, hid)
    back, dgate, dup, gated = expert_part(rows, scales, gate_codes, up_codes, down_codes, chunk)
    summed = lax.psum_scatter(back, "blk", scatter_dimension=0, tiled=True)
    gate_grad, up_grad, down_grad = grads_part(rows, dgate, dup, gated, width, chunk)
    summed, gate_grad, up_grad, down_grad = lax.optimization_barrier(
        (summed, gate_grad, up_grad, down_grad)
    )
    home = lax.all_to_all(
        summed.reshape(experts, capacity, -1), "eg", split_axis=0, concat_axis=0, tiled=True
    ).reshape(slots, -1)
    grad_tokens = jnp.dot(flat, home[:, :width], preferred_element_type=f32).astype(bf16)
    home_scores = home[:, width].astype(f32)
    grad_gates = jnp.sum(flat_picked * home_scores[None, None, :], axis=2).astype(bf16)
    return (grad_tokens, grad_gates, gate_grad, up_grad, down_grad)


def solution(mesh):
    in_specs = (
        P(("eg", "blk"), None),
        P(("eg", "blk"), None),
        P(("eg", "blk"), None),
        P(("eg", "blk"), None),
        P("eg", None, "blk"),
        P("eg", None, "blk"),
        P("eg", None, "blk"),
        P("eg", None, "blk", None),
    )
    out_specs = (
        P(("eg", "blk"), None),
        P(("eg", "blk"), None),
        P("eg", None, "blk"),
        P("eg", None, "blk"),
        P("eg", None, "blk"),
    )
    return jax.shard_map(
        on_device, mesh=mesh, in_specs=in_specs, out_specs=out_specs, check_vma=False
    )
```

time: 233 us -> 154 us (0.66)
  local copies, waits for them, and re-layouts: 73.7 us -> 5.79 us
  matrix products: 55.2 us -> 2.21 us
  blocking collectives: 12.4 us -> 49.2 us
  waiting for transfers between devices: 14.3 us -> 49.4 us
  starting transfers between devices: 31 us -> 0.08 us
  Pallas kernels: 0 us -> 29.1 us
  other arithmetic: 30.5 us -> 3.22 us
    dot_general x11 -> x2, matrix products: 55.2 us -> 2.21 us  [the longest x1 1.32 us: on_device(): lax.dot_general(flat, both, TN, preferred_element_type=f32).astype(bf16)]
    all_to_all x0 -> x2, blocking collectives: none -> 49.2 us  [the longest x1 30.5 us: on_device(): lax.all_to_all(sent.reshape(experts, capacity, -1), 'eg', split_axis=0, c...]
    convert_element_type x8 -> x5, local copies, waits for them, and re-layouts: 43.5 us -> 0.46 us  [the longest x2 0.19 us: on_device(): gates.astype(bf16)[:, None]]
    all_to_all x5 -> x0, starting transfers between devices: 30.9 us -> none  [the longest x1 7.25 us: on_device(): lax.all_to_all(send_tokens, 'eg', split_axis=0, concat_axis=0, tiled=True)]
    all_gather x2 -> x1, waiting for transfers between devices: 0.04 us -> 29.9 us  [on_device(): lax.all_gather(received.reshape(slots, -1), 'blk', axis=0, tiled=True)]
    pallas_call x0 -> x2, Pallas kernels: none -> 29.1 us  [the longest x1 18.4 us: expert_part(): pl.pallas_call(functools.partial(expert_kernel, steps), grid=(steps,), in...]
    convert_element_type x4, other arithmetic: 28.5 us -> 0.85 us  [the longest x1 0.66 us: on_device(): gate_weights.astype(f32)[:, :, None]]
    reduce_scatter x0 -> x1, waiting for transfers between devices: none -> 19.5 us  [on_device(): summed = lax.psum_scatter(back, 'blk', scatter_dimension=0, tiled=True)]
  transfers between devices with their start and end apart: 8 -> 2, of which waited for: 2 -> 2; matrix products, arithmetic and copies ran while one was open for 46% -> 0% of each run, Pallas kernels for 0% -> 7%
where the time goes in v1:
time: 154 us; the launch traced here: 153 us
  waiting for transfers between devices  49.4 us (32%)
  blocking collectives  49.2 us (32%)
  Pallas kernels  29.1 us (19%)
  between operations  14.1 us (9%)
  local copies, waits for them, and re-layouts  5.79 us (4%)
  other arithmetic  3.22 us (2%)
  matrix products  2.21 us (1%)
    all_to_all x1, blocking collectives, on_device(): lax.all_to_all(sent.reshape(experts, capacity, -1), 'eg', split_axis=0, c...  30.5 us
    all_gather x1, waiting for transfers between devices, on_device(): lax.all_gather(received.reshape(slots, -1), 'blk', axis=0, tiled=True)  29.9 us
    reduce_scatter x1, waiting for transfers between devices, on_device(): summed = lax.psum_scatter(back, 'blk', scatter_dimension=0, tiled=True)  19.5 us
    all_to_all x1, blocking collectives, on_device(): lax.all_to_all(summed.reshape(experts, capacity, -1), 'eg', split_axis=0,...  18.7 us
    pallas_call x1, Pallas kernels, expert_part(): pl.pallas_call(functools.partial(expert_kernel, steps), grid=(steps,), in...  18.4 us
    pallas_call x1, Pallas kernels, grads_part(): pl.pallas_call(grads_kernel, grid=(steps,), in_specs=[pl.BlockSpec((count...  10.7 us
  transfers between devices with their start and end apart: 2, of which 2 were waited for; matrix products, arithmetic and copies ran while one was open for 0% of the time, Pallas kernels for 7%

profile of v1, /device:TPU:0, one launch (start us, length us, event | category | flops | bytes accessed | tf_op | source)
XLA Modules:
  0.0 153.2 jit_solution(6035970082503501964)
XLA Ops:
  7.2 0.0 copy-start.3
  7.2 0.0 all-gather.2.cloned.1.call-start
  7.2 0.8 fusion.7
  8.0 0.7 fusion.5
  8.7 0.7 convert_element_type.83
  9.4 0.1 copy.24
  9.5 0.1 multiply_reduce_fusion.2
  9.6 0.1 copy.23
  9.6 0.1 eq.51
  9.7 0.1 copy.25
  9.8 0.1 multiply_reduce_fusion.1
  9.9 0.1 copy.26
  10.0 0.1 convert_element_type.85
  10.1 0.1 convert_convert_fusion
  10.2 1.3 convolution_convert_fusion
  11.5 0.1 broadcast_in_dim.4
  11.6 0.1 pad_maximum_fusion
  11.6 0.2 reshape.82
  11.9 30.5 %all_to_all.10 = bf16[8,4,14464]{2,1,0:T(4,128)(2,1)S(1)} all-to-all(bf16[8,4,14464]{2,1,0:T(4,128)(2,1)S(1)} %reshape.82), channel_id=1, replica_groups=mesh['eg'=8,'blk'=4] {'eg'}, dimensions={0} | all-to-all | bytes 1851392 | tf_op jit(solution)/shard_map/all_to_all | solution.py:194
  42.4 1.1 reshape.83
  43.5 0.0 all-gather.2.cloned.1.call-update
  43.5 0.0 reduce-scatter.2.cloned.1.call-start
  43.6 0.0 copy-done.3
  43.6 0.1 copy.27
  43.7 0.2 broadcast_in_dim.5
  44.0 0.1 reshape_reshape.3
  44.2 29.9 %all-gather.2.cloned.1.call-done.x_ref.y_ref.gates_ref = bf16[128,14464]{1,0:T(8,128)(2,1)} async-done(((bf16[32,14464]{1,0:T(8,128)(2,1)}), bf16[128,14464]{1,0:T(8,128)(2,1)}) %all-gather.2.cloned.1.call-update) | async-done | bytes 3702800 | tf_op jit(solution)/shard_map/all_gather | solution.py:197
  74.1 18.4 %expert.1 = (bf16[128,7296]{1,0:T(8,128)(2,1)}, bf16[128,512]{1,0:T(8,128)(2,1)S(1)}, bf16[128,512]{1,0:T(8,128)(2,1)S(1)}, bf16[128,512]{1,0:T(8,128)(2,1)S(1)}) custom-call(bf16[128,14464]{1,0:T(8,128)(2,1)} %all-gather.2.cloned.1.call-done.x_ref.y_ref.gates_ref, bf16[128,14464]{1,0:T(8,128)(2,1)} %all-gather.2.cloned.1.call-done.x_ref.y_ref.gates_ref, ...), custom_call_target="tpu_custom_call" | custom-call | flops 4697620480 | bytes 27525120 | tf_op jit(solution)/shard_map/expert/pallas_call | solution.py:120
  92.5 0.0 copy-start
  92.5 0.6 copy-done
  93.1 0.0 copy-start.1
  93.1 0.6 copy-done.1
  93.8 0.0 copy-start.2
  93.8 0.7 copy-done.2
  94.4 0.0 reduce-scatter.2.cloned.1.call-update
  94.5 10.7 %grads.1 = (bf16[1,7168,512]{2,1,0:T(8,128)(2,1)}, bf16[1,7168,512]{2,1,0:T(8,128)(2,1)}, bf16[1,7168,512]{2,1,0:T(8,128)(2,1)}) custom-call(bf16[128,14464]{1,0:T(8,128)(2,1)} %all-gather.2.cloned.1.call-done.x_ref.y_ref.gates_ref, bf16[128,14464]{1,0:T(8,128)(2,1)} %all-gather.2.cloned.1.call-done.x_ref.y_ref.gates_ref, bf16[128,512]{1,0:T(8,128)(2,1)} %copy-done, ...), custom_call_target="tpu_custom_call" | custom-call | flops 2818572288 | bytes 25690112 | tf_op jit(solution)/shard_map/grads/pallas_call | solution.py:155
  105.2 19.5 %reduce-scatter.2.cloned.1.call-done = bf16[32,7296]{1,0:T(8,128)(2,1)} async-done(((bf16[128,7296]{1,0:T(8,128)(2,1)}), bf16[32,7296]{1,0:T(8,128)(2,1)}) %reduce-scatter.2.cloned.1.call-update) | async-done | bytes 466960 | tf_op jit(solution)/shard_map/reduce_scatter | solution.py:204
  124.6 1.1 reshape.85
  125.8 18.7 %all_to_all.11 = bf16[8,4,7296]{2,1,0:T(4,128)(2,1)S(1)} all-to-all(bf16[8,4,7296]{2,1,0:T(4,128)(2,1)S(1)} %reshape.85), channel_id=1, replica_groups=mesh['eg'=8,'blk'=4] {'eg'}, dimensions={0} | all-to-all | bytes 933888 | tf_op jit(solution)/shard_map/all_to_all | solution.py:209
  144.5 0.1 reshape.86
  144.6 0.1 convert_reduce_fusion
  144.7 0.9 convolution_convert_fusion.1
  145.6 0.1 reshape.87
  145.7 0.1 copy.29
  145.7 0.6 multiply_reduce_fusion
  (7 shorter events, 0.1 us)
Async XLA Ops:
  7.2 36.4 %copy-start.3 = (bf16[1,3,4,56]{3,2,1,0:T(4,128)(2,1)S(1)}, bf16[1,3,4,56]{3,2,1,0:T(4,128)(2,1)}, u32[]{:S(2)}) copy-start(bf16[1,3,4,56]{3,2,1,0:T(4,128)(2,1)} %param.15) | copy-start | bytes 4036
  7.2 66.9 %all-gather.2.cloned.1.call-start = ((), (), s32[]{:S(2)}) async-start(), calls=%async_computation.3 | async-start | bytes 4628480 | tf_op jit(solution)/shard_map/all_gather | solution.py:197
  43.5 81.1 %reduce-scatter.2.cloned.1.call-start = ((), (), s32[]{:S(2)}) async-start(), calls=%async_computation.4 | async-start | bytes 2334720 | tf_op jit(solution)/shard_map/reduce_scatter | solution.py:204
  92.5 0.7 copy-start
  93.1 0.6 copy-start.1
  93.8 0.7 copy-start.2
Sparse Core Ops, SparseCore 0:
  43.7 30.3 all-gather.1
  94.6 29.9 reduce-scatter.1

commit v2 on v1

--- a/solution.py
+++ b/solution.py
@@ -108,12 +108,12 @@
     ).astype(bf16)
 
 
-def expert_part(rows, scales, gate_codes, up_codes, down_codes, chunk):
+def expert_part(rows, cotan, scales, gate_codes, up_codes, down_codes, chunk):
     count = rows.shape[0]
     _, width, hid = gate_codes.shape
     steps = width // chunk
     x_spec = pl.BlockSpec((count, chunk), lambda j: (0, j))
-    y_spec = pl.BlockSpec((count, chunk), lambda j: (0, steps + j))
+    y_spec = pl.BlockSpec((count, chunk), lambda j: (0, j))
     code_spec = pl.BlockSpec((1, chunk, hid), lambda j: (0, j, 0))
     whole = pl.BlockSpec((count, hid), lambda j: (0, 0))
     small = jax.ShapeDtypeStruct((count, hid), bf16)
@@ -123,7 +123,7 @@
         in_specs=[
             x_spec,
             y_spec,
-            pl.BlockSpec((count, LANES), lambda j: (0, 2 * width // LANES)),
+            pl.BlockSpec((count, LANES), lambda j: (0, width // LANES)),
             pl.BlockSpec((1, scales.shape[1], hid), lambda j: (j, 0, 0)),
             code_spec,
             code_spec,
@@ -144,10 +144,10 @@
             transcendentals=count * hid,
         ),
         name="expert",
-    )(rows, rows, rows, scales, gate_codes, up_codes, down_codes)
-
-
-def grads_part(rows, dgate, dup, gated, width, chunk):
+    )(rows, cotan, cotan, scales, gate_codes, up_codes, down_codes)
+
+
+def grads_part(rows, cotan, dgate, dup, gated, width, chunk):
     count, hid = dgate.shape
     steps = width // chunk
     whole = pl.BlockSpec((count, hid), lambda j: (0, 0))
@@ -157,7 +157,7 @@
         grid=(steps,),
         in_specs=[
             pl.BlockSpec((count, chunk), lambda j: (0, j)),
-            pl.BlockSpec((count, chunk), lambda j: (0, steps + j)),
+            pl.BlockSpec((count, chunk), lambda j: (0, j)),
             whole,
             whole,
             whole,
@@ -171,7 +171,7 @@
             transcendentals=0,
         ),
         name="grads",
-    )(rows, rows, dgate, dup, gated)
+    )(rows, cotan, dgate, dup, gated)
 
 
 def on_device(
@@ -186,23 +186,30 @@
     flat = placed.astype(bf16).reshape(-1, slots)
     flat_picked = picked.reshape(-1, TOPK, slots)
     gates = jnp.sum(flat_picked * gate_weights.astype(f32)[:, :, None], axis=(0, 1))
-    both = jnp.concatenate([tokens, grad_out], axis=1)
-    sent = lax.dot_general(flat, both, TN, preferred_element_type=f32).astype(bf16)
+
+    def exchange(sent):
+        received = lax.all_to_all(
+            sent.reshape(experts, capacity, -1), "eg", split_axis=0, concat_axis=0, tiled=True
+        )
+        return received.reshape(slots, -1)
+
+    sent = lax.dot_general(flat, tokens, TN, preferred_element_type=f32).astype(bf16)
+    received = exchange(sent)
+    sent = lax.dot_general(flat, grad_out, TN, preferred_element_type=f32).astype(bf16)
     sent = jnp.concatenate(
         [sent, jnp.broadcast_to(gates.astype(bf16)[:, None], (slots, LANES))], axis=1
     )
-    received = lax.all_to_all(
-        sent.reshape(experts, capacity, -1), "eg", split_axis=0, concat_axis=0, tiled=True
-    )
-    rows = lax.all_gather(received.reshape(slots, -1), "blk", axis=0, tiled=True)
+    received, sent = lax.optimization_barrier((received, sent))
+    rows = lax.all_gather(received, "blk", axis=0, tiled=True)
+    cotan = lax.all_gather(exchange(sent), "blk", axis=0, tiled=True)
 
     hid = gate_codes.shape[2]
     scales = jnp.repeat(jnp.swapaxes(block_scales[0], 1, 2).astype(f32), QBLOCK, axis=2)
     scales = scales.reshape(3, width // chunk, chunk // QBLOCK, hid)
     scales = jnp.swapaxes(scales, 0, 1).reshape(width // chunk, -1, hid)
-    back, dgate, dup, gated = expert_part(rows, scales, gate_codes, up_codes, down_codes, chunk)
+    back, dgate, dup, gated = expert_part(rows, cotan, scales, gate_codes, up_codes, down_codes, chunk)
     summed = lax.psum_scatter(back, "blk", scatter_dimension=0, tiled=True)
-    gate_grad, up_grad, down_grad = grads_part(rows, dgate, dup, gated, width, chunk)
+    gate_grad, up_grad, down_grad = grads_part(rows, cotan, dgate, dup, gated, width, chunk)
     summed, gate_grad, up_grad, down_grad = lax.optimization_barrier(
         (summed, gate_grad, up_grad, down_grad)
     )

time: 154 us -> 155 us (level)
  blocking collectives: 49.2 us -> 35.5 us
  starting transfers between devices: 0.08 us -> 7.37 us
  waiting for transfers between devices: 49.4 us -> 54.9 us
  local copies, waits for them, and re-layouts: 5.79 us -> 8.79 us
    all_to_all x1, blocking collectives: 30.5 us -> 16.9 us  [exchange(): lax.all_to_all(sent.reshape(experts, capacity, -1), 'eg', split_axis=0, c...]
    all_to_all x0 -> x1, waiting for transfers between devices: none -> 9.99 us  [exchange(): lax.all_to_all(sent.reshape(experts, capacity, -1), 'eg', split_axis=0, c...]
    all_to_all x0 -> x1, starting transfers between devices: none -> 7.25 us  [exchange(): lax.all_to_all(sent.reshape(experts, capacity, -1), 'eg', split_axis=0, c...]
    all_gather x1 -> x2, waiting for transfers between devices: 29.9 us -> 25.3 us  [the longest x1 23.5 us: on_device(): cotan = lax.all_gather(exchange(sent), 'blk', axis=0, tiled=True)]
    unnamed x8 -> x12, local copies, waits for them, and re-layouts: 1.95 us -> 3.5 us
  transfers between devices with their start and end apart: 2 -> 4, of which waited for: 2 -> 4; matrix products, arithmetic and copies ran while one was open for 0% -> 3% of each run, Pallas kernels for 7% -> 7%
where the time goes in v2:
time: 155 us
  waiting for transfers between devices  54.9 us (35%)
  blocking collectives  35.5 us (23%)
  Pallas kernels  28.7 us (19%)
  between operations  13.9 us (9%)
  local copies, waits for them, and re-layouts  8.79 us (6%)
  starting transfers between devices  7.37 us (5%)
  other arithmetic  3.23 us (2%)
  matrix products  2.29 us (1%)
    all_gather x1, waiting for transfers between devices, on_device(): cotan = lax.all_gather(exchange(sent), 'blk', axis=0, tiled=True)  23.5 us
    reduce_scatter x1, waiting for transfers between devices, on_device(): summed = lax.psum_scatter(back, 'blk', scatter_dimension=0, tiled=True)  19.5 us
    all_to_all x1, blocking collectives, on_device(): lax.all_to_all(summed.reshape(experts, capacity, -1), 'eg', split_axis=0,...  18.7 us
    pallas_call x1, Pallas kernels, expert_part(): pl.pallas_call(functools.partial(expert_kernel, steps), grid=(steps,), in...  18 us
    all_to_all x1, blocking collectives, exchange(): lax.all_to_all(sent.reshape(experts, capacity, -1), 'eg', split_axis=0, c...  16.9 us
    pallas_call x1, Pallas kernels, grads_part(): pl.pallas_call(grads_kernel, grid=(steps,), in_specs=[pl.BlockSpec((count...  10.7 us
    all_to_all x1, waiting for transfers between devices, exchange(): lax.all_to_all(sent.reshape(experts, capacity, -1), 'eg', split_axis=0, c...  9.99 us
    all_to_all x1, starting transfers between devices, exchange(): lax.all_to_all(sent.reshape(experts, capacity, -1), 'eg', split_axis=0, c...  7.25 us
  transfers between devices with their start and end apart: 4, of which 4 were waited for; matrix products, arithmetic and copies ran while one was open for 3% of the time, Pallas kernels for 7%

profile of v2, /device:TPU:0, one launch (start us, length us, event | category | flops | bytes accessed | tf_op | source)
XLA Modules:
  0.0 154.6 jit_solution(451669648243960404)
XLA Ops:
  7.2 0.8 fusion.4
  8.0 0.1 copy.24
  8.1 0.1 multiply_reduce_fusion.2
  8.2 0.1 copy.23
  8.2 0.1 eq.51
  8.3 0.1 convert_convert_fusion
  8.4 0.2 convolution_convert_fusion.1
  8.7 0.9 reshape.88
  9.6 7.3 %all-to-all-start = ((bf16[8,4,7168]{2,1,0:T(4,128)(2,1)}), bf16[8,4,7168]{2,1,0:T(4,128)(2,1)S(1)}, u32[]{:S(2)}, u32[]{:S(2)}) async-start(bf16[8,4,7168]{2,1,0:T(4,128)(2,1)} %reshape.88), calls=%async_computation | async-start | bytes 917504 | tf_op jit(solution)/shard_map/all_to_all | solution.py:191
  16.9 0.0 all-gather.3.cloned.1.call-start
  16.9 0.8 fusion.2
  17.7 0.7 convert_element_type.87
  18.3 0.1 copy.25
  18.4 0.1 multiply_reduce_fusion.1
  18.5 0.1 copy.26
  18.6 0.1 convert_element_type.89
  18.7 1.1 convolution_convert_fusion
  19.8 0.1 broadcast_in_dim.4
  20.0 10.0 %all-to-all-done = bf16[8,4,7168]{2,1,0:T(4,128)(2,1)S(1)} async-done(((bf16[8,4,7168]{2,1,0:T(4,128)(2,1)}), bf16[8,4,7168]{2,1,0:T(4,128)(2,1)S(1)}, u32[]{:S(2)}, u32[]{:S(2)}) %all-to-all-start) | async-done | bytes 458784 | tf_op jit(solution)/shard_map/all_to_all | solution.py:191
  29.9 0.9 reshape.89
  30.8 0.0 all-gather.3.cloned.1.call-update
  30.8 0.0 all-gather.5.cloned.1.call-start
  30.9 0.1 reshape.90
  31.0 16.9 %all_to_all.15 = bf16[8,4,7296]{2,1,0:T(4,128)(2,1)S(1)} all-to-all(bf16[8,4,7296]{2,1,0:T(4,128)(2,1)S(1)} %reshape.90), channel_id=1, replica_groups=mesh['eg'=8,'blk'=4] {'eg'}, dimensions={0} | all-to-all | bytes 933888 | tf_op jit(solution)/shard_map/all_to_all | solution.py:191
  47.9 0.9 reshape.91
  48.7 0.0 all-gather.5.cloned.1.call-update
  48.8 0.0 reduce-scatter.2.cloned.1.call-start
  48.8 0.1 copy.27
  48.9 0.2 broadcast_in_dim.5
  49.2 0.1 reshape_reshape.3
  49.4 1.8 %all-gather.3.cloned.1.call-done.x_ref = bf16[128,7168]{1,0:T(8,128)(2,1)} async-done(((bf16[32,7168]{1,0:T(8,128)(2,1)}), bf16[128,7168]{1,0:T(8,128)(2,1)}) %all-gather.3.cloned.1.call-update) | async-done | bytes 1835024 | tf_op jit(solution)/shard_map/all_gather | solution.py:203
  51.2 23.5 %all-gather.5.cloned.1.call-done.y_ref.gates_ref = bf16[128,7296]{1,0:T(8,128)(2,1)} async-done(((bf16[32,7296]{1,0:T(8,128)(2,1)}), bf16[128,7296]{1,0:T(8,128)(2,1)}) %all-gather.5.cloned.1.call-update) | async-done | bytes 1867792 | tf_op jit(solution)/shard_map/all_gather | solution.py:204
  74.7 1.5 copy-done.1
  76.2 18.0 %expert.1 = (bf16[128,7296]{1,0:T(8,128)(2,1)}, bf16[128,512]{1,0:T(8,128)(2,1)S(1)}, bf16[128,512]{1,0:T(8,128)(2,1)S(1)}, bf16[128,512]{1,0:T(8,128)(2,1)S(1)}) custom-call(bf16[128,7168]{1,0:T(8,128)(2,1)S(1)} %copy-done.1, bf16[128,7296]{1,0:T(8,128)(2,1)} %all-gather.5.cloned.1.call-done.y_ref.gates_ref, ...), custom_call_target="tpu_custom_call" | custom-call | flops 4697620480 | bytes 27525120 | tf_op jit(solution)/shard_map/expert/pallas_call | solution.py:120
  94.2 0.7 copy-done.2
  94.9 0.7 copy-done.3
  95.6 0.7 copy-done.4
  96.2 0.0 reduce-scatter.2.cloned.1.call-update
  96.2 10.7 %grads.1 = (bf16[1,7168,512]{2,1,0:T(8,128)(2,1)}, bf16[1,7168,512]{2,1,0:T(8,128)(2,1)}, bf16[1,7168,512]{2,1,0:T(8,128)(2,1)}) custom-call(bf16[128,7168]{1,0:T(8,128)(2,1)} %all-gather.3.cloned.1.call-done.x_ref, bf16[128,7296]{1,0:T(8,128)(2,1)} %all-gather.5.cloned.1.call-done.y_ref.gates_ref, bf16[128,512]{1,0:T(8,128)(2,1)} %copy-done.2, ...), custom_call_target="tpu_custom_call" | custom-call | flops 2818572288 | bytes 25690112 | tf_op jit(solution)/shard_map/grads/pallas_call | solution.py:155
  106.9 19.5 %reduce-scatter.2.cloned.1.call-done = bf16[32,7296]{1,0:T(8,128)(2,1)} async-done(((bf16[128,7296]{1,0:T(8,128)(2,1)}), bf16[32,7296]{1,0:T(8,128)(2,1)}) %reduce-scatter.2.cloned.1.call-update) | async-done | bytes 466960 | tf_op jit(solution)/shard_map/reduce_scatter | solution.py:211
  126.4 1.1 reshape.93
  127.6 18.7 %all_to_all.16 = bf16[8,4,7296]{2,1,0:T(4,128)(2,1)S(1)} all-to-all(bf16[8,4,7296]{2,1,0:T(4,128)(2,1)S(1)} %reshape.93), channel_id=1, replica_groups=mesh['eg'=8,'blk'=4] {'eg'}, dimensions={0} | all-to-all | bytes 933888 | tf_op jit(solution)/shard_map/all_to_all | solution.py:216
  146.2 0.1 reshape.94
  146.3 0.1 convert_reduce_fusion
  146.4 0.9 convolution_convert_fusion.2
  147.3 0.1 reshape.95
  147.4 0.1 copy.29
  147.5 0.6 multiply_reduce_fusion
  (16 shorter events, 0.1 us)
Async XLA Ops:
  7.2 1.2 copy-start
  7.2 41.6 %copy-start.5 = (bf16[1,3,4,56]{3,2,1,0:T(4,128)(2,1)S(1)}, bf16[1,3,4,56]{3,2,1,0:T(4,128)(2,1)}, u32[]{:S(2)}) copy-start(bf16[1,3,4,56]{3,2,1,0:T(4,128)(2,1)} %param.15) | copy-start | bytes 4036
  9.6 20.3 %all-to-all-start = ((bf16[8,4,7168]{2,1,0:T(4,128)(2,1)}), bf16[8,4,7168]{2,1,0:T(4,128)(2,1)S(1)}, u32[]{:S(2)}, u32[]{:S(2)}) async-start(bf16[8,4,7168]{2,1,0:T(4,128)(2,1)} %reshape.88), calls=%async_computation | async-start | bytes 917504 | tf_op jit(solution)/shard_map/all_to_all | solution.py:191
  16.9 34.3 %all-gather.3.cloned.1.call-start = ((), (), s32[]{:S(2)}) async-start(), calls=%async_computation.4 | async-start | bytes 2293760 | tf_op jit(solution)/shard_map/all_gather | solution.py:203
  30.8 43.8 %all-gather.5.cloned.1.call-start = ((), (), s32[]{:S(2)}) async-start(), calls=%async_computation.5 | async-start | bytes 2334720 | tf_op jit(solution)/shard_map/all_gather | solution.py:204
  48.8 77.7 %reduce-scatter.2.cloned.1.call-start = ((), (), s32[]{:S(2)}) async-start(), calls=%async_computation.6 | async-start | bytes 2334720 | tf_op jit(solution)/shard_map/reduce_scatter | solution.py:211
  74.7 1.5 copy-start.1
  94.2 0.7 copy-start.2
  94.9 0.7 copy-start.3
  95.5 0.7 copy-start.4
Sparse Core Ops, SparseCore 0:
  31.0 20.1 all-gather.2
  53.3 21.2 all-gather.4
  96.3 30.0 reduce-scatter.1

commit v3 on v2

--- a/solution.py
+++ b/solution.py
@@ -174,6 +174,34 @@
     )(rows, cotan, dgate, dup, gated)
 
 
+def shifted(value, step):
+    count = lax.axis_size("blk")
+    return lax.ppermute(value, "blk", [(i, (i + 2 * step) % count) for i in range(count)])
+
+
+def other_core(value):
+    count = lax.axis_size("blk")
+    return lax.ppermute(value, "blk", [(i, i ^ 1) for i in range(count)])
+
+
+def gather_rows(own):
+    chips = lax.axis_size("blk") // 2
+    mine = jnp.concatenate([own] + [shifted(own, step) for step in range(1, chips)], axis=0)
+    return jnp.concatenate([mine, other_core(mine)], axis=0)
+
+
+def return_rows(back):
+    chips = lax.axis_size("blk") // 2
+    half = back.shape[0] // 2
+    size = half // chips
+    sums = back[:half].astype(f32) + other_core(back[half:]).astype(f32)
+    sums = sums.astype(bf16)
+    total = sums[:size].astype(f32)
+    for step in range(1, chips):
+        total += shifted(sums[step * size : (step + 1) * size], -step).astype(f32)
+    return total.astype(bf16)
+
+
 def on_device(
     tokens, grad_out, expert_ids, gate_weights, gate_codes, up_codes, down_codes, block_scales
 ):
@@ -200,15 +228,15 @@
         [sent, jnp.broadcast_to(gates.astype(bf16)[:, None], (slots, LANES))], axis=1
     )
     received, sent = lax.optimization_barrier((received, sent))
-    rows = lax.all_gather(received, "blk", axis=0, tiled=True)
-    cotan = lax.all_gather(exchange(sent), "blk", axis=0, tiled=True)
+    rows = gather_rows(received)
+    cotan = gather_rows(exchange(sent))
 
     hid = gate_codes.shape[2]
     scales = jnp.repeat(jnp.swapaxes(block_scales[0], 1, 2).astype(f32), QBLOCK, axis=2)
     scales = scales.reshape(3, width // chunk, chunk // QBLOCK, hid)
     scales = jnp.swapaxes(scales, 0, 1).reshape(width // chunk, -1, hid)
     back, dgate, dup, gated = expert_part(rows, cotan, scales, gate_codes, up_codes, down_codes, chunk)
-    summed = lax.psum_scatter(back, "blk", scatter_dimension=0, tiled=True)
+    summed = return_rows(back)
     gate_grad, up_grad, down_grad = grads_part(rows, cotan, dgate, dup, gated, width, chunk)
     summed, gate_grad, up_grad, down_grad = lax.optimization_barrier(
         (summed, gate_grad, up_grad, down_grad)

time: 155 us -> 112 us (0.72)
  blocking collectives: 35.5 us -> 18.4 us
  waiting for transfers between devices: 54.9 us -> 37.9 us
  between operations: 13.9 us -> 0.97 us
  starting transfers between devices: 7.37 us -> 15.9 us
  local copies, waits for them, and re-layouts: 8.79 us -> 6.37 us
    ppermute x0 -> x6, waiting for transfers between devices: none -> 26 us  [the longest x3 22.5 us: shifted(): lax.ppermute(value, 'blk', [(i, (i + 2 * step) % count) for i in range(co...]
    all_gather x2 -> x0, waiting for transfers between devices: 25.3 us -> none  [the longest x1 23.5 us: on_device(): cotan = lax.all_gather(exchange(sent), 'blk', axis=0, tiled=True)]
    reduce_scatter x1 -> x0, waiting for transfers between devices: 19.5 us -> none  [on_device(): summed = lax.psum_scatter(back, 'blk', scatter_dimension=0, tiled=True)]
    all_to_all x1 -> x0, blocking collectives: 16.9 us -> none  [exchange(): lax.all_to_all(sent.reshape(experts, capacity, -1), 'eg', split_axis=0, c...]
    ppermute x0 -> x6, starting transfers between devices: none -> 5.02 us  [the longest x3 4.75 us: shifted(): lax.ppermute(value, 'blk', [(i, (i + 2 * step) % count) for i in range(co...]
    all_to_all x1 -> x2, starting transfers between devices: 7.25 us -> 10.9 us  [exchange(): lax.all_to_all(sent.reshape(experts, capacity, -1), 'eg', split_axis=0, c...]
    unnamed x12 -> x24, local copies, waits for them, and re-layouts: 3.5 us -> 1.43 us
    all_to_all x1 -> x2, waiting for transfers between devices: 9.99 us -> 11.9 us  [exchange(): lax.all_to_all(sent.reshape(experts, capacity, -1), 'eg', split_axis=0, c...]
  transfers between devices with their start and end apart: 4 -> 8, of which waited for: 4 -> 7; matrix products, arithmetic and copies ran while one was open for 3% -> 3% of each run, Pallas kernels for 7% -> 9%
where the time goes in v3:
time: 112 us
  waiting for transfers between devices  37.9 us (34%)
  Pallas kernels  27.3 us (24%)
  blocking collectives  18.4 us (16%)
  starting transfers between devices  15.9 us (14%)
  local copies, waits for them, and re-layouts  6.37 us (6%)
  other arithmetic  3.27 us (3%)
  matrix products  1.38 us (1%)
    ppermute x3, waiting for transfers between devices, shifted(): lax.ppermute(value, 'blk', [(i, (i + 2 * step) % count) for i in range(co...  22.5 us
    all_to_all x1, blocking collectives, on_device(): lax.all_to_all(summed.reshape(experts, capacity, -1), 'eg', split_axis=0,...  18.4 us
    pallas_call x1, Pallas kernels, expert_part(): pl.pallas_call(functools.partial(expert_kernel, steps), grid=(steps,), in...  16.8 us
    all_to_all x2, waiting for transfers between devices, exchange(): lax.all_to_all(sent.reshape(experts, capacity, -1), 'eg', split_axis=0, c...  11.9 us
    all_to_all x2, starting transfers between devices, exchange(): lax.all_to_all(sent.reshape(experts, capacity, -1), 'eg', split_axis=0, c...  10.9 us
    pallas_call x1, Pallas kernels, grads_part(): pl.pallas_call(grads_kernel, grid=(steps,), in_specs=[pl.BlockSpec((count...  10.5 us
    ppermute x3, starting transfers between devices, shifted(): lax.ppermute(value, 'blk', [(i, (i + 2 * step) % count) for i in range(co...  4.75 us
    ppermute x3, waiting for transfers between devices, other_core(): return lax.ppermute(value, 'blk', [(i, i ^ 1) for i in range(count)])  3.54 us
  transfers between devices with their start and end apart: 8, of which 7 were waited for; matrix products, arithmetic and copies ran while one was open for 3% of the time, Pallas kernels for 9%

profile of v3, /device:TPU:0, one launch (start us, length us, event | category | flops | bytes accessed | tf_op | source)
XLA Modules:
  0.0 111.6 jit_solution(14642609822144664852)
XLA Ops:
  0.7 0.8 fusion.4
  1.5 0.1 copy.24
  1.6 0.1 multiply_reduce_fusion.2
  1.7 0.1 eq.51
  1.8 0.1 convert_convert_fusion
  1.9 0.2 convolution_convert_fusion.1
  2.2 0.9 reshape.88
  3.1 7.3 %all-to-all-start = ((bf16[8,4,7168]{2,1,0:T(4,128)(2,1)}), bf16[8,4,7168]{2,1,0:T(4,128)(2,1)S(1)}, u32[]{:S(2)}, u32[]{:S(2)}) async-start(bf16[8,4,7168]{2,1,0:T(4,128)(2,1)} %reshape.88), calls=%async_computation | async-start | bytes 917504 | tf_op jit(solution)/shard_map/all_to_all | solution.py:219
  10.5 0.1 copy.25
  10.6 0.1 multiply_reduce_fusion.1
  10.7 0.1 copy.26
  10.8 0.1 convert_element_type.107
  10.9 0.1 copy.27
  11.0 0.2 broadcast_in_dim.5
  11.2 0.1 reshape_reshape.3
  11.4 0.2 convolution_convert_fusion
  11.7 0.1 broadcast_in_dim.4
  11.8 11.7 %all-to-all-done = bf16[8,4,7168]{2,1,0:T(4,128)(2,1)S(1)} async-done(((bf16[8,4,7168]{2,1,0:T(4,128)(2,1)}), bf16[8,4,7168]{2,1,0:T(4,128)(2,1)S(1)}, u32[]{:S(2)}, u32[]{:S(2)}) %all-to-all-start) | async-done | bytes 458784 | tf_op jit(solution)/shard_map/all_to_all | solution.py:219
  23.4 0.1 reshape.89
  23.6 0.9 reshape.90
  24.4 3.6 %all-to-all-start.1 = ((bf16[8,4,7296]{2,1,0:T(4,128)(2,1)}), bf16[8,4,7296]{2,1,0:T(4,128)(2,1)S(1)}, u32[]{:S(2)}, u32[]{:S(2)}) async-start(bf16[8,4,7296]{2,1,0:T(4,128)(2,1)} %reshape.90), calls=%async_computation.1 | async-start | bytes 933888 | tf_op jit(solution)/shard_map/all_to_all | solution.py:219
  28.1 1.5 %collective-permute-start = (bf16[32,7168]{1,0:T(8,128)(2,1)S(1)}, bf16[32,7168]{1,0:T(8,128)(2,1)S(1)}, u32[]{:S(2)}, u32[]{:S(2)}) collective-permute-start(bf16[32,7168]{1,0:T(8,128)(2,1)S(1)} %reshape.89), channel_id=1, source_target_pairs={{0,2},{1,3},{2,0},{3,1},{4,6},{5,7},{6,4},{7,5},{8,10},{9,11},{10,... | collective-permute-start | bytes 1376264 | tf_op jit(solution)/shard_map/ppermute | solution.py:179
  29.6 10.5 %collective-permute-done = bf16[32,7168]{1,0:T(8,128)(2,1)S(1)} collective-permute-done((bf16[32,7168]{1,0:T(8,128)(2,1)S(1)}, bf16[32,7168]{1,0:T(8,128)(2,1)S(1)}, u32[]{:S(2)}, u32[]{:S(2)}) %collective-permute-start) | collective-permute-done | bytes 458784 | tf_op jit(solution)/shard_map/ppermute | solution.py:179
  40.1 1.0 pad_maximum_fusion.1
  41.2 0.3 all-to-all-done.1
  41.4 0.1 reshape.91
  41.5 1.6 %collective-permute-start.2 = (bf16[32,7296]{1,0:T(8,128)(2,1)S(1)}, bf16[32,7296]{1,0:T(8,128)(2,1)S(1)}, u32[]{:S(2)}, u32[]{:S(2)}) collective-permute-start(bf16[32,7296]{1,0:T(8,128)(2,1)S(1)} %reshape.91), channel_id=1, source_target_pairs={{0,2},{1,3},{2,0},{3,1},{4,6},{5,7},{6,4},{7,5},{8,10},{9,11},{10,... | collective-permute-start | bytes 1400840 | tf_op jit(solution)/shard_map/ppermute | solution.py:179
  43.2 11.3 %collective-permute-done.2 = bf16[32,7296]{1,0:T(8,128)(2,1)S(1)} collective-permute-done((bf16[32,7296]{1,0:T(8,128)(2,1)S(1)}, bf16[32,7296]{1,0:T(8,128)(2,1)S(1)}, u32[]{:S(2)}, u32[]{:S(2)}) %collective-permute-start.2) | collective-permute-done | bytes 466976 | tf_op jit(solution)/shard_map/ppermute | solution.py:179
  54.7 1.2 %constant_dynamic-update-slice_fusion.x_ref = bf16[128,7168]{1,0:T(8,128)(2,1)S(1)} fusion(bf16[128,7168]{1,0:T(8,128)(2,1)S(1)} %constant_dynamic-update-slice_fusion.1, bf16[64,7168]{1,0:T(8,128)(2,1)} %collective-permute-done.1), kind=kLoop, calls=%fused_computation.17 | loop fusion | bytes 1835008 | tf_op jit(solution)/shard_map/concatenate | solution.py:190
  55.9 1.2 %collective-permute-done.3 = bf16[64,7296]{1,0:T(8,128)(2,1)S(1)} collective-permute-done((bf16[64,7296]{1,0:T(8,128)(2,1)S(1)}, bf16[64,7296]{1,0:T(8,128)(2,1)S(1)}, u32[]{:S(2)}, u32[]{:S(2)}) %collective-permute-start.3) | collective-permute-done | bytes 933920 | tf_op jit(solution)/shard_map/ppermute | solution.py:184
  57.1 0.1 constant_dynamic-update-slice_fusion.3.y_ref.gates_ref
  57.2 1.2 %copy-done.5 = bf16[128,7296]{1,0:T(8,128)(2,1)} copy-done((bf16[128,7296]{1,0:T(8,128)(2,1)}, bf16[128,7296]{1,0:T(8,128)(2,1)S(1)}, u32[]{:S(2)}) %copy-start.5) | copy-done | bytes 1867800
  58.5 16.8 %expert.1 = (bf16[128,7296]{1,0:T(8,128)(2,1)S(1)}, bf16[128,512]{1,0:T(8,128)(2,1)S(1)}, bf16[128,512]{1,0:T(8,128)(2,1)S(1)}, bf16[128,512]{1,0:T(8,128)(2,1)S(1)}) custom-call(bf16[128,7168]{1,0:T(8,128)(2,1)S(1)} %constant_dynamic-update-slice_fusion.x_ref, bf16[128,7296]{1,0:T(8,128)(2,1)} %copy-done.5, bf16[128,7296]{1,0:T(8,128)(2,1)} %copy-done.5, ...), custom_call_target="tpu_custom_call" | custom-call | flops 4697620480 | bytes 27525120 | tf_op jit(solution)/shard_map/expert/pallas_call | solution.py:120
  75.4 0.2 collective-permute-start.4
  75.6 2.4 %collective-permute-done.4 = bf16[64,7296]{1,0:T(8,128)(2,1)S(1)} collective-permute-done((bf16[64,7296]{1,0:T(8,128)(2,1)S(1)}, bf16[64,7296]{1,0:T(8,128)(2,1)S(1)}, u32[]{:S(2)}, u32[]{:S(2)}) %collective-permute-start.4) | collective-permute-done | bytes 933920 | tf_op jit(solution)/shard_map/ppermute | solution.py:184
  77.9 0.2 add_convert_fusion
  78.2 1.6 %collective-permute-start.5 = (bf16[32,7296]{1,0:T(8,128)(2,1)S(1)}, bf16[32,7296]{1,0:T(8,128)(2,1)S(1)}, u32[]{:S(2)}, u32[]{:S(2)}) collective-permute-start(bf16[32,7296]{1,0:T(8,128)(2,1)S(1)} %slice.25), channel_id=1, source_target_pairs={{0,2},{1,3},{2,0},{3,1},{4,6},{5,7},{6,4},{7,5},{8,10},{9,11},{10,... | collective-permute-start | bytes 1400840 | tf_op jit(solution)/shard_map/ppermute | solution.py:179
  79.9 10.5 %grads.1 = (bf16[1,7168,512]{2,1,0:T(8,128)(2,1)}, bf16[1,7168,512]{2,1,0:T(8,128)(2,1)}, bf16[1,7168,512]{2,1,0:T(8,128)(2,1)}) custom-call(bf16[128,7168]{1,0:T(8,128)(2,1)} %copy-done.1, bf16[128,7296]{1,0:T(8,128)(2,1)} %copy-done.5, bf16[128,512]{1,0:T(8,128)(2,1)} %copy-done.2, bf16[128,512]{1,0:T(8,128)(2,1)} %copy-done.3, bf16[128,512]{1,0:T(8,128)(2,1)} %copy-done.4), custom_call_target="tpu_custom_call" | custom-call | flops 2818572288 | bytes 25690112 | tf_op jit(solution)/shard_map/grads/pallas_call | solution.py:155
  90.4 0.6 collective-permute-done.5
  91.0 0.1 add_convert_fusion.1
  91.2 0.1 reshape.93
  91.3 18.4 %all_to_all.15 = bf16[8,4,7296]{2,1,0:T(4,128)(2,1)S(1)} all-to-all(bf16[8,4,7296]{2,1,0:T(4,128)(2,1)S(1)} %reshape.93), channel_id=1, replica_groups=mesh['eg'=8,'blk'=4] {'eg'}, dimensions={0} | all-to-all | bytes 933888 | tf_op jit(solution)/shard_map/all_to_all | solution.py:244
  109.7 0.1 reshape.94
  109.8 0.1 convert_reduce_fusion
  109.9 0.9 convolution_convert_fusion.2
  110.8 0.1 reshape.95
  110.9 0.1 copy.29
  111.0 0.6 multiply_reduce_fusion
  (40 shorter events, 0.6 us)
Async XLA Ops:
  0.6 1.3 %copy-start = (bf16[8,7168]{1,0:T(8,128)(2,1)S(1)}, bf16[8,7168]{1,0:T(8,128)(2,1)}, u32[]{:S(2)}) copy-start(bf16[8,7168]{1,0:T(8,128)(2,1)} %param.8) | copy-start | bytes 344068
  0.6 9.7 %copy-start.7 = (s32[8,2]{0,1:T(2,128)S(1)}, s32[8,2]{0,1:T(2,128)}, u32[]{:S(2)}) copy-start(s32[8,2]{0,1:T(2,128)} %param.10) | copy-start | bytes 196
  0.7 9.8 %copy-start.9 = (bf16[8,2]{0,1:T(2,128)(2,1)S(1)}, bf16[8,2]{0,1:T(2,128)(2,1)}, u32[]{:S(2)}) copy-start(bf16[8,2]{0,1:T(2,128)(2,1)} %param.11) | copy-start | bytes 100
  0.7 9.8 %copy-start.8 = (bf16[1,3,4,56]{3,2,1,0:T(4,128)(2,1)S(1)}, bf16[1,3,4,56]{3,2,1,0:T(4,128)(2,1)}, u32[]{:S(2)}) copy-start(bf16[1,3,4,56]{3,2,1,0:T(4,128)(2,1)} %param.15) | copy-start | bytes 4036
  2.2 9.2 %copy-start.6 = (bf16[8,7168]{1,0:T(8,128)(2,1)S(1)}, bf16[8,7168]{1,0:T(8,128)(2,1)}, u32[]{:S(2)}) copy-start(bf16[8,7168]{1,0:T(8,128)(2,1)} %param.9) | copy-start | bytes 344068
  3.1 20.3 %all-to-all-start = ((bf16[8,4,7168]{2,1,0:T(4,128)(2,1)}), bf16[8,4,7168]{2,1,0:T(4,128)(2,1)S(1)}, u32[]{:S(2)}, u32[]{:S(2)}) async-start(bf16[8,4,7168]{2,1,0:T(4,128)(2,1)} %reshape.88), calls=%async_computation | async-start | bytes 917504 | tf_op jit(solution)/shard_map/all_to_all | solution.py:219
  24.4 17.0 %all-to-all-start.1 = ((bf16[8,4,7296]{2,1,0:T(4,128)(2,1)}), bf16[8,4,7296]{2,1,0:T(4,128)(2,1)S(1)}, u32[]{:S(2)}, u32[]{:S(2)}) async-start(bf16[8,4,7296]{2,1,0:T(4,128)(2,1)} %reshape.90), calls=%async_computation.1 | async-start | bytes 933888 | tf_op jit(solution)/shard_map/all_to_all | solution.py:219
  28.1 12.1 %collective-permute-start = (bf16[32,7168]{1,0:T(8,128)(2,1)S(1)}, bf16[32,7168]{1,0:T(8,128)(2,1)S(1)}, u32[]{:S(2)}, u32[]{:S(2)}) collective-permute-start(bf16[32,7168]{1,0:T(8,128)(2,1)S(1)} %reshape.89), channel_id=1, source_target_pairs={{0,2},{1,3},{2,0},{3,1},{4,6},{5,7},{6,4},{7,5},{8,10},{9,11},{10,... | collective-permute-start | bytes 1376264 | tf_op jit(solution)/shard_map/ppermute | solution.py:179
  41.1 13.5 %collective-permute-start.1 = (bf16[64,7168]{1,0:T(8,128)(2,1)}, bf16[64,7168]{1,0:T(8,128)(2,1)}, u32[]{:S(2)}, u32[]{:S(2)}) collective-permute-start(bf16[64,7168]{1,0:T(8,128)(2,1)} %pad_maximum_fusion.1), channel_id=1, source_target_pairs={{0,1},{1,0},{2,3},{3,2},{4,5},{5,4},{6,7},{7,6},{8,9},{9,8},{10,11... | collective-permute-start | bytes 2752520 | tf_op jit(solution)/shard_map/ppermute | solution.py:184
  41.5 12.9 %collective-permute-start.2 = (bf16[32,7296]{1,0:T(8,128)(2,1)S(1)}, bf16[32,7296]{1,0:T(8,128)(2,1)S(1)}, u32[]{:S(2)}, u32[]{:S(2)}) collective-permute-start(bf16[32,7296]{1,0:T(8,128)(2,1)S(1)} %reshape.91), channel_id=1, source_target_pairs={{0,2},{1,3},{2,0},{3,1},{4,6},{5,7},{6,4},{7,5},{8,10},{9,11},{10,... | collective-permute-start | bytes 1400840 | tf_op jit(solution)/shard_map/ppermute | solution.py:179
  54.5 2.6 %collective-permute-start.3 = (bf16[64,7296]{1,0:T(8,128)(2,1)S(1)}, bf16[64,7296]{1,0:T(8,128)(2,1)S(1)}, u32[]{:S(2)}, u32[]{:S(2)}) collective-permute-start(bf16[64,7296]{1,0:T(8,128)(2,1)S(1)} %pad_maximum_fusion), channel_id=1, source_target_pairs={{0,1},{1,0},{2,3},{3,2},{4,5},{5,4},{6,7},{7,6},{8,9},{9,8},{10,11... | collective-permute-start | bytes 2801672 | tf_op jit(solution)/shard_map/ppermute | solution.py:184
  55.9 19.4 %copy-start.1 = (bf16[128,7168]{1,0:T(8,128)(2,1)}, bf16[128,7168]{1,0:T(8,128)(2,1)S(1)}, u32[]{:S(2)}) copy-start(bf16[128,7168]{1,0:T(8,128)(2,1)S(1)} %constant_dynamic-update-slice_fusion.x_ref) | copy-start | bytes 5505028
  57.2 1.3 %copy-start.5 = (bf16[128,7296]{1,0:T(8,128)(2,1)}, bf16[128,7296]{1,0:T(8,128)(2,1)S(1)}, u32[]{:S(2)}) copy-start(bf16[128,7296]{1,0:T(8,128)(2,1)S(1)} %constant_dynamic-update-slice_fusion.3.y_ref.gates_ref) | copy-start | bytes 5603332
  75.3 2.9 %copy-start.2 = (bf16[128,512]{1,0:T(8,128)(2,1)}, bf16[128,512]{1,0:T(8,128)(2,1)S(1)}, u32[]{:S(2)}) copy-start(bf16[128,512]{1,0:T(8,128)(2,1)S(1)} %get-tuple-element.21.dgate_ref) | copy-start | bytes 393220
  75.3 2.9 %copy-start.3 = (bf16[128,512]{1,0:T(8,128)(2,1)}, bf16[128,512]{1,0:T(8,128)(2,1)S(1)}, u32[]{:S(2)}) copy-start(bf16[128,512]{1,0:T(8,128)(2,1)S(1)} %get-tuple-element.22.dup_ref) | copy-start | bytes 393220
  75.3 2.9 %copy-start.4 = (bf16[128,512]{1,0:T(8,128)(2,1)}, bf16[128,512]{1,0:T(8,128)(2,1)S(1)}, u32[]{:S(2)}) copy-start(bf16[128,512]{1,0:T(8,128)(2,1)S(1)} %get-tuple-element.23.gated_ref) | copy-start | bytes 393220
  75.4 2.6 %collective-permute-start.4 = (bf16[64,7296]{1,0:T(8,128)(2,1)S(1)}, bf16[64,7296]{1,0:T(8,128)(2,1)S(1)}, u32[]{:S(2)}, u32[]{:S(2)}) collective-permute-start(bf16[64,7296]{1,0:T(8,128)(2,1)S(1)} %slice.19), channel_id=1, source_target_pairs={{0,1},{1,0},{2,3},{3,2},{4,5},{5,4},{6,7},{7,6},{8,9},{9,8},{10,11... | collective-permute-start | bytes 2801672 | tf_op jit(solution)/shard_map/ppermute | solution.py:184
  78.2 12.8 %collective-permute-start.5 = (bf16[32,7296]{1,0:T(8,128)(2,1)S(1)}, bf16[32,7296]{1,0:T(8,128)(2,1)S(1)}, u32[]{:S(2)}, u32[]{:S(2)}) collective-permute-start(bf16[32,7296]{1,0:T(8,128)(2,1)S(1)} %slice.25), channel_id=1, source_target_pairs={{0,2},{1,3},{2,0},{3,1},{4,6},{5,7},{6,4},{7,5},{8,10},{9,11},{10,... | collective-permute-start | bytes 1400840 | tf_op jit(solution)/shard_map/ppermute | solution.py:179
